TPU v7x, 1024 devices: a whole 4x8x16 slice. The times are simulated.
1024 devices in a mesh: mem: 64 (over y, x, core), reg: 16 (over z).
Axes of the slice: x: 4, y: 8, z: 16, core: 2. Of those that a mesh axis runs over, the one named last changes fastest.
Arguments:
- ens_state: bfloat16 [1024, 524288], P('mem', 'reg'), may hold values from -6 to 6
- ens_obs: bfloat16 [1024, 262144], P('mem', 'reg'), may hold values from -6 to 6
- innov: bfloat16 [1024, 262144], P('mem', 'reg'), may hold values from -6 to 6
- state_coord: int32 [2, 524288], P(None, 'reg'), may hold values from 0 to 63
- obs_coord: int32 [2, 262144], replicated, may hold values from 0 to 63
- obs_routes: int32 [2048, 1], replicated, may hold values from 0 to 15; in each aligned block of 128 rows (0 to 127, 128 to 255, ...) at most 16 rows name the same one
Outputs:
- analysis: bfloat16 [1024, 524288], P('mem', 'reg')
Inputs may be any that keep to these rules, and one draw needn't show every extreme that they name: `obs_routes`: in each aligned block of 128 rows (the observation blocks of one source region) no region is named by more than 16 rows, a bound that some block reaches.
All inputs are finite; a program needn't handle non-finite values.
Results may differ from a plain program's by a relative error of at most 0.0022.
The roundings to bfloat16 on the way count: a program that leaves them out, or rounds other values in their place, can miss the bound.
Values may be sent and summed in bfloat16 or wider, within the bound.
A program may use at most 32 MiB of HBM per device.

v0:
```python
import jax
import jax.numpy as jnp
from jax import lax
from jax.sharding import PartitionSpec as P

BLK = 128
LOC = 32
SLOTS = 4


def slot_table(routes, regions, per_region, capacity):
    target = routes[:, 0].reshape(regions, per_region)
    hits = (target[:, :, None] == jnp.arange(regions, dtype=jnp.int32)[None, None, :]).astype(
        jnp.int32
    )
    order = jnp.cumsum(hits, axis=1) - 1
    chosen = hits[:, :, :, None] * (
        order[:, :, :, None] == jnp.arange(capacity, dtype=jnp.int32)[None, None, None, :]
    ).astype(jnp.int32)
    listed = jnp.sum(chosen * jnp.arange(per_region, dtype=jnp.int32)[None, :, None, None], axis=1)
    filled = jnp.sum(chosen, axis=1)
    return (listed, filled)


def taper_weight(dist_sq):
    ratio = jnp.sqrt(dist_sq) / LOC
    clipped = jnp.maximum(ratio, 1.0)
    inner = (((-0.25 * ratio + 0.5) * ratio + 0.625) * ratio - 5.0 / 3.0) * ratio * ratio + 1.0
    outer = (
        ((((ratio / 12.0 - 0.5) * ratio + 0.625) * ratio + 5.0 / 3.0) * ratio - 5.0) * ratio
        + 4.0
        - 2.0 / (3.0 * clipped)
    )
    return jnp.where(ratio <= 1.0, inner, jnp.where(ratio < 2.0, outer, 0.0))


def per_device(ens_state, ens_obs, innov, state_coord, obs_coord, obs_routes):
    regions = lax.axis_size("reg")
    bands = lax.axis_size("mem")
    region_idx = lax.axis_index("reg")
    band_idx = lax.axis_index("mem")
    mem_dev = ens_state.shape[0]
    members = mem_dev * bands
    per_region = ens_obs.shape[1] // BLK
    capacity = SLOTS * bands // regions
    listed, filled = slot_table(obs_routes, regions, per_region, capacity)
    state_wide = ens_state.astype(jnp.float32)
    state_total, obs_total = lax.psum(
        (jnp.sum(state_wide, axis=0), jnp.sum(ens_obs.astype(jnp.float32), axis=0)), "mem"
    )
    state_send = (state_wide - state_total[None, :] / members).astype(jnp.bfloat16)
    obs_source = (ens_obs.astype(jnp.float32) - obs_total[None, :] / members).astype(jnp.bfloat16)
    send_ids = listed[region_idx].reshape(-1)
    send_mask = filled[region_idx].reshape(-1).astype(jnp.bfloat16)
    obs_pick = (
        jnp.take(obs_source.reshape(mem_dev, per_region, BLK), send_ids, axis=1)
        * send_mask[None, :, None]
    ).reshape(mem_dev, -1)
    innov_pick = (
        jnp.take(innov.reshape(mem_dev, per_region, BLK), send_ids, axis=1)
        * send_mask[None, :, None]
    ).reshape(mem_dev, -1)
    obs_recv, innov_recv = (
        lax.all_to_all(obs_pick, "reg", split_axis=1, concat_axis=1, tiled=True),
        lax.all_to_all(innov_pick, "reg", split_axis=1, concat_axis=1, tiled=True),
    )
    state_rows = lax.all_to_all(state_send, "mem", split_axis=1, concat_axis=0, tiled=True)
    obs_rows, innov_rows = (
        lax.all_to_all(obs_recv, "mem", split_axis=1, concat_axis=0, tiled=True),
        lax.all_to_all(innov_recv, "mem", split_axis=1, concat_axis=0, tiled=True),
    )
    band_rows = state_rows.shape[1]
    rows_xy = lax.dynamic_slice_in_dim(state_coord, band_idx * band_rows, band_rows, 1)
    slot_ids = band_idx * SLOTS + jnp.arange(SLOTS, dtype=jnp.int32)
    source = slot_ids // capacity
    column = slot_ids % capacity
    block_ids = source * per_region + listed[source, region_idx, column]
    obs_xy = jnp.take(obs_coord.reshape(2, -1, BLK), block_ids, axis=1).reshape(2, -1)
    cov = lax.dot_general(
        state_rows, obs_rows, (((0,), (0,)), ((), ())), preferred_element_type=jnp.float32
    ) / (members - 1)
    delta_x = rows_xy[0][:, None] - obs_xy[0][None, :]
    delta_y = rows_xy[1][:, None] - obs_xy[1][None, :]
    dist_sq = (delta_x * delta_x + delta_y * delta_y).astype(jnp.float32)
    tiles = (cov * taper_weight(dist_sq)).astype(jnp.bfloat16)
    increments = lax.dot_general(
        innov_rows, tiles, (((1,), (1,)), ((), ())), preferred_element_type=jnp.float32
    ).astype(jnp.bfloat16)
    returned = lax.all_to_all(increments, "mem", split_axis=0, concat_axis=1, tiled=True)
    return (state_wide + returned.astype(jnp.float32)).astype(jnp.bfloat16)


def solution(mesh):
    return jax.shard_map(
        per_device,
        mesh=mesh,
        in_specs=(P("mem", "reg"), P("mem", "reg"), P("mem", "reg"), P(None, "reg"), P(), P()),
        out_specs=P("mem", "reg"),
        check_vma=False,
    )
```

profile of v0, /device:TPU:1, one launch (start us, length us, event | category | flops | bytes accessed | tf_op | source)
XLA Modules:
  0.0 513.3 jit_solution(14792977575824652798)
XLA Ops:
  6.5 2.0 convert_reduce_fusion.1
  8.5 2.2 convert_reduce_fusion
  14.2 1.6 copy.54
  17.4 212.4 %all-reduce.3.cloned.1.call-done = (f32[16384]{0:T(1024)}, f32[32768]{0:T(1024)}) async-done(((f32[16384]{0:T(1024)}, f32[32768]{0:T(1024)}), (f32[16384]{0:T(1024)}, f32[32768]{0:T(1024)})) %all-reduce.3.cloned.1.call-update) | async-done | bytes 196624 | tf_op jit(solution)/shard_map/psum | solution.py:48
  232.1 9.7 %all-to-all-start.2 = ((bf16[16,64,512]{2,0,1:T(8,128)(2,1)}), bf16[16,64,512]{2,0,1:T(8,128)(2,1)}, u32[]{:S(2)}, u32[]{:S(2)}) async-start(bf16[16,64,512]{2,0,1:T(8,128)(2,1)} %bitcast.65), calls=%async_computation.2 | async-start | bytes 2097152 | tf_op jit(solution)/shard_map/all_to_all | solution.py:67
  241.8 8.7 %select_reduce_fusion = (s32[16,16,16]{2,1,0:T(8,128)S(1)}, s32[16,16,16]{2,1,0:T(8,128)S(1)}) fusion(s32[16,128,16]{1,2,0:T(8,128)S(1)} %copy.55, s32[16,128,16]{1,2,0:T(8,128)S(1)} %copy.54), kind=kLoop, calls=%fused_computation.7 | loop fusion | flops 2613248 | bytes 294912 | tf_op jit(solution)/shard_map/reduce_sum | solution.py:21
  250.7 1.9 copy_bitcast_fusion.2
  252.6 2.8 gather_fusion.2
  255.5 1.9 copy_bitcast_fusion.1
  257.4 2.8 gather_fusion.3
  260.2 3.6 bitcast_multiply_fusion
  265.0 2.3 all_to_all.69
  267.3 2.8 copy.64
  270.1 13.0 %all-to-all-start.3 = ((bf16[16,16,2048]{2,0,1:T(8,128)(2,1)}), bf16[16,16,2048]{2,0,1:T(8,128)(2,1)}, u32[]{:S(2)}, u32[]{:S(2)}) async-start(bf16[16,16,2048]{2,0,1:T(8,128)(2,1)} %copy.64), calls=%async_computation.3 | async-start | bytes 2097152 | tf_op jit(solution)/shard_map/all_to_all | solution.py:64
  283.1 2.5 copy.57
  285.6 2.3 all_to_all.60
  287.9 2.8 copy.58
  290.7 36.8 %all-to-all-done.3 = bf16[16,16,2048]{2,0,1:T(8,128)(2,1)} async-done(((bf16[16,16,2048]{2,0,1:T(8,128)(2,1)}), bf16[16,16,2048]{2,0,1:T(8,128)(2,1)}, u32[]{:S(2)}, u32[]{:S(2)}) %all-to-all-start.3) | async-done | bytes 1048608 | tf_op jit(solution)/shard_map/all_to_all | solution.py:64
  327.5 13.7 %all-to-all-start = ((bf16[16,16,2048]{2,0,1:T(8,128)(2,1)}), bf16[16,16,2048]{2,0,1:T(8,128)(2,1)}, u32[]{:S(2)}, u32[]{:S(2)}) async-start(bf16[16,16,2048]{2,0,1:T(8,128)(2,1)} %copy.58), calls=%async_computation | async-start | bytes 2097152 | tf_op jit(solution)/shard_map/all_to_all | solution.py:65
  341.2 2.8 copy.65
  344.0 2.5 all_to_all.71
  346.5 2.8 copy.66
  349.3 37.2 %all-to-all-done = bf16[16,16,2048]{2,0,1:T(8,128)(2,1)} async-done(((bf16[16,16,2048]{2,0,1:T(8,128)(2,1)}), bf16[16,16,2048]{2,0,1:T(8,128)(2,1)}, u32[]{:S(2)}, u32[]{:S(2)}) %all-to-all-start) | async-done | bytes 1048608 | tf_op jit(solution)/shard_map/all_to_all | solution.py:65
  386.5 15.8 %all-to-all-start.4 = ((bf16[16,64,512]{2,0,1:T(8,128)(2,1)}), bf16[16,64,512]{2,0,1:T(8,128)(2,1)}, u32[]{:S(2)}, u32[]{:S(2)}) async-start(bf16[16,64,512]{2,0,1:T(8,128)(2,1)} %copy.66), calls=%async_computation.4 | async-start | bytes 2097152 | tf_op jit(solution)/shard_map/all_to_all | solution.py:69
  402.3 2.8 copy.59
  405.0 2.5 all_to_all.62
  407.5 2.8 copy.60
  410.3 19.9 %all-to-all-done.4 = bf16[16,64,512]{2,0,1:T(8,128)(2,1)} async-done(((bf16[16,64,512]{2,0,1:T(8,128)(2,1)}), bf16[16,64,512]{2,0,1:T(8,128)(2,1)}, u32[]{:S(2)}, u32[]{:S(2)}) %all-to-all-start.4) | async-done | bytes 1048608 | tf_op jit(solution)/shard_map/all_to_all | solution.py:69
  430.2 6.7 %all-to-all-start.1 = ((bf16[16,64,512]{2,0,1:T(8,128)(2,1)}), bf16[16,64,512]{2,0,1:T(8,128)(2,1)}, u32[]{:S(2)}, u32[]{:S(2)}) async-start(bf16[16,64,512]{2,0,1:T(8,128)(2,1)} %copy.60), calls=%async_computation.1 | async-start | bytes 2097152 | tf_op jit(solution)/shard_map/all_to_all | solution.py:70
  439.1 25.7 %all-to-all-done.1 = bf16[16,64,512]{2,0,1:T(8,128)(2,1)} async-done(((bf16[16,64,512]{2,0,1:T(8,128)(2,1)}), bf16[16,64,512]{2,0,1:T(8,128)(2,1)}, u32[]{:S(2)}, u32[]{:S(2)}) %all-to-all-start.1) | async-done | bytes 1048608 | tf_op jit(solution)/shard_map/all_to_all | solution.py:70
  464.7 5.5 %convolution_convert_fusion = bf16[1024,512]{1,0:T(8,128)(2,1)} fusion(bf16[1024,512]{1,0:T(8,128)(2,1)} %bitcast.3, bf16[16,64,512]{2,0,1:T(8,128)(2,1)} %all-to-all-done.4, bf16[16,64,512]{2,0,1:T(8,128)(2,1)} %all-to-all-done.2, s32[512]{0:T(512)S(1)} %bitcast.72, s32[512]{0:T(512)S(1)} %bitcast.70, s32[512]{0:T(512)S(1)} %bitcast.71, s32[512]{0:T(512)S(1)} %bitcast.69), kind=kOutput, calls=%fused_computation.15 | convolution fusion | flops 1083965440 | bytes 4202496 | tf_op jit(solution)/shard_map/dot_general | solution.py:86
  470.3 34.4 %all_to_all.82 = bf16[64,16,512]{2,1,0:T(8,128)(2,1)S(1)} all-to-all(bf16[64,16,512]{2,1,0:T(8,128)(2,1)} %bitcast.67), channel_id=1, replica_groups=mesh['mem'=64,'reg'=16] {'mem'}, dimensions={0} | all-to-all | bytes 2097152 | tf_op jit(solution)/shard_map/all_to_all | solution.py:89
  (36 shorter events, 12.7 us)
Async XLA Ops:
  6.5 431.0 %copy-start = (s32[2,262144]{1,0:T(2,128)S(1)}, s32[2,262144]{1,0:T(2,128)}, u32[]{:S(2)}) copy-start(s32[2,262144]{1,0:T(2,128)} %param.12) | copy-start | bytes 6291460
  6.5 223.2 %all-reduce.3.cloned.1.call-start = ((), (), s32[]{:S(2)}) async-start(), calls=%async_computation.6 | async-start | bytes 393216 | tf_op jit(solution)/shard_map/psum | solution.py:48
  12.9 217.8 %copy-start.1 = (bf16[16,32768]{1,0:T(8,128)(2,1)S(1)}, bf16[16,32768]{1,0:T(8,128)(2,1)}, u32[]{:S(2)}) copy-start(bf16[16,32768]{1,0:T(8,128)(2,1)} %param.8) | copy-start | bytes 3145732
  232.1 38.0 %all-to-all-start.2 = ((bf16[16,64,512]{2,0,1:T(8,128)(2,1)}), bf16[16,64,512]{2,0,1:T(8,128)(2,1)}, u32[]{:S(2)}, u32[]{:S(2)}) async-start(bf16[16,64,512]{2,0,1:T(8,128)(2,1)} %bitcast.65), calls=%async_computation.2 | async-start | bytes 2097152 | tf_op jit(solution)/shard_map/all_to_all | solution.py:67
  250.5 5.0 copy-start.2
  270.1 57.4 %all-to-all-start.3 = ((bf16[16,16,2048]{2,0,1:T(8,128)(2,1)}), bf16[16,16,2048]{2,0,1:T(8,128)(2,1)}, u32[]{:S(2)}, u32[]{:S(2)}) async-start(bf16[16,16,2048]{2,0,1:T(8,128)(2,1)} %copy.64), calls=%async_computation.3 | async-start | bytes 2097152 | tf_op jit(solution)/shard_map/all_to_all | solution.py:64
  327.5 59.0 %all-to-all-start = ((bf16[16,16,2048]{2,0,1:T(8,128)(2,1)}), bf16[16,16,2048]{2,0,1:T(8,128)(2,1)}, u32[]{:S(2)}, u32[]{:S(2)}) async-start(bf16[16,16,2048]{2,0,1:T(8,128)(2,1)} %copy.58), calls=%async_computation | async-start | bytes 2097152 | tf_op jit(solution)/shard_map/all_to_all | solution.py:65
  386.5 43.7 %all-to-all-start.4 = ((bf16[16,64,512]{2,0,1:T(8,128)(2,1)}), bf16[16,64,512]{2,0,1:T(8,128)(2,1)}, u32[]{:S(2)}, u32[]{:S(2)}) async-start(bf16[16,64,512]{2,0,1:T(8,128)(2,1)} %copy.66), calls=%async_computation.4 | async-start | bytes 2097152 | tf_op jit(solution)/shard_map/all_to_all | solution.py:69
  430.2 34.6 %all-to-all-start.1 = ((bf16[16,64,512]{2,0,1:T(8,128)(2,1)}), bf16[16,64,512]{2,0,1:T(8,128)(2,1)}, u32[]{:S(2)}, u32[]{:S(2)}) async-start(bf16[16,64,512]{2,0,1:T(8,128)(2,1)} %copy.60), calls=%async_computation.1 | async-start | bytes 2097152 | tf_op jit(solution)/shard_map/all_to_all | solution.py:70
Sparse Core Ops, SparseCore 0:
  10.9 218.8 all-reduce.2
where the time goes:
time: 515 us; the launch traced here: 513 us
  waiting for transfers between devices  332 us (64%)
  starting transfers between devices  58.8 us (11%)
  local copies, waits for them, and re-layouts  45.1 us (9%)
  blocking collectives  34.4 us (7%)
  other arithmetic  23.8 us (5%)
  between operations  13.5 us (3%)
  matrix products  5.52 us (1%)
    psum x1, waiting for transfers between devices, per_device(): lax.psum((jnp.sum(state_wide, axis=0), jnp.sum(ens_obs.astype(jnp.float32...  212 us
    all_to_all x1, waiting for transfers between devices, per_device(): lax.all_to_all(innov_pick, 'reg', split_axis=1, concat_axis=1, tiled=True)  37.2 us
    all_to_all x1, waiting for transfers between devices, per_device(): lax.all_to_all(obs_pick, 'reg', split_axis=1, concat_axis=1, tiled=True)  36.8 us
    all_to_all x1, blocking collectives, per_device(): lax.all_to_all(increments, 'mem', split_axis=0, concat_axis=1, tiled=True)  34.4 us
    all_to_all x1, waiting for transfers between devices, per_device(): lax.all_to_all(innov_recv, 'mem', split_axis=1, concat_axis=0, tiled=True)  25.7 us
    all_to_all x1, waiting for transfers between devices, per_device(): lax.all_to_all(obs_recv, 'mem', split_axis=1, concat_axis=0, tiled=True)  19.9 us
    all_to_all x1, starting transfers between devices, per_device(): lax.all_to_all(obs_recv, 'mem', split_axis=1, concat_axis=0, tiled=True)  15.8 us
    all_to_all x1, starting transfers between devices, per_device(): lax.all_to_all(innov_pick, 'reg', split_axis=1, concat_axis=1, tiled=True)  13.7 us
  transfers between devices with their start and end apart: 6, of which 5 were waited for; matrix products, arithmetic and copies ran while one was open for 10% of the time, Pallas kernels for 0%

commit v1 on v0

v1 whole, which is shorter than its diff:
```python
import jax
import jax.numpy as jnp
from jax import lax
from jax.sharding import PartitionSpec as P

BLK = 128
LOC = 32
SLOTS = 4


def slots_of(target, wanted):
    k = jnp.arange(target.shape[0], dtype=jnp.int32)
    earlier = (target[None, :] == target[:, None]) & (k[None, :] < k[:, None])
    rank = jnp.sum(earlier.astype(jnp.int32), axis=1)
    return (target[None, :] == wanted[0][:, None]) & (rank[None, :] == wanted[1][:, None])


def taper_weight(dist_sq):
    ratio = jnp.sqrt(dist_sq) / LOC
    clipped = jnp.maximum(ratio, 1.0)
    inner = (((-0.25 * ratio + 0.5) * ratio + 0.625) * ratio - 5.0 / 3.0) * ratio * ratio + 1.0
    outer = (
        ((((ratio / 12.0 - 0.5) * ratio + 0.625) * ratio + 5.0 / 3.0) * ratio - 5.0) * ratio
        + 4.0
        - 2.0 / (3.0 * clipped)
    )
    return jnp.where(ratio <= 1.0, inner, jnp.where(ratio < 2.0, outer, 0.0))


def anomaly(rows):
    wide = rows.astype(jnp.float32)
    return (wide - jnp.mean(wide, axis=0, keepdims=True)).astype(jnp.bfloat16)


def per_device(ens_state, ens_obs, innov, state_coord, obs_coord, obs_routes):
    regions = lax.axis_size("reg")
    bands = lax.axis_size("mem")
    region_idx = lax.axis_index("reg")
    band_idx = lax.axis_index("mem")
    mem_dev = ens_state.shape[0]
    members = mem_dev * bands
    per_region = ens_obs.shape[1] // BLK
    capacity = SLOTS * bands // regions
    wide = SLOTS * BLK
    state_rows = lax.all_to_all(ens_state, "mem", split_axis=1, concat_axis=0, tiled=True)
    routes = obs_routes[:, 0]
    target = lax.dynamic_slice_in_dim(routes, region_idx * per_region, per_region)
    q = jnp.arange(regions * capacity, dtype=jnp.int32)
    hot = slots_of(target, (q // capacity, q % capacity)).astype(jnp.bfloat16)
    both = jnp.stack([ens_obs, innov]).reshape(2, mem_dev, per_region, BLK)
    pick = jnp.einsum(
        "gsk,amkx->gamsx",
        hot.reshape(bands, SLOTS, per_region),
        both,
        preferred_element_type=jnp.float32,
    ).astype(jnp.bfloat16)
    pick = pick.reshape(regions, bands // regions * 2 * mem_dev, wide)
    recv = lax.all_to_all(pick, "reg", split_axis=0, concat_axis=0, tiled=True)
    recv = recv.reshape(bands, 2 * mem_dev, wide)
    rows = lax.all_to_all(recv, "mem", split_axis=0, concat_axis=0, tiled=True)
    rows = rows.reshape(bands, 2, mem_dev, wide)
    obs_rows = rows[:, 0].reshape(members, wide)
    innov_rows = rows[:, 1].reshape(members, wide)
    band_rows = state_rows.shape[1]
    rows_xy = lax.dynamic_slice_in_dim(state_coord, band_idx * band_rows, band_rows, 1)
    slot_ids = band_idx * SLOTS + jnp.arange(SLOTS, dtype=jnp.int32)
    source = band_idx * SLOTS // capacity
    theirs = lax.dynamic_slice_in_dim(routes, source * per_region, per_region)
    here = slots_of(theirs, (jnp.full((SLOTS,), region_idx), slot_ids % capacity)).astype(jnp.int32)
    filled = jnp.sum(here, axis=1)
    block_ids = source * per_region + jnp.sum(here * jnp.arange(per_region, dtype=jnp.int32), axis=1)
    obs_xy = jnp.concatenate(
        [lax.dynamic_slice_in_dim(obs_coord, block_ids[s] * BLK, BLK, 1) for s in range(SLOTS)], axis=1
    )
    cov = lax.dot_general(
        anomaly(state_rows), anomaly(obs_rows), (((0,), (0,)), ((), ())), preferred_element_type=jnp.float32
    ) / (members - 1)
    delta_x = rows_xy[0][:, None] - obs_xy[0][None, :]
    delta_y = rows_xy[1][:, None] - obs_xy[1][None, :]
    dist_sq = (delta_x * delta_x + delta_y * delta_y).astype(jnp.float32)
    present = jnp.repeat(filled, BLK).astype(jnp.float32)
    tiles = (cov * (taper_weight(dist_sq) * present[None, :])).astype(jnp.bfloat16)
    increments = lax.dot_general(
        innov_rows, tiles, (((1,), (1,)), ((), ())), preferred_element_type=jnp.float32
    ).astype(jnp.bfloat16)
    returned = lax.all_to_all(increments, "mem", split_axis=0, concat_axis=1, tiled=True)
    return (ens_state.astype(jnp.float32) + returned.astype(jnp.float32)).astype(jnp.bfloat16)


def solution(mesh):
    return jax.shard_map(
        per_device,
        mesh=mesh,
        in_specs=(P("mem", "reg"), P("mem", "reg"), P("mem", "reg"), P(None, "reg"), P(), P()),
        out_specs=P("mem", "reg"),
        check_vma=False,
    )
```

time: 515 us -> 258 us (0.50)
  waiting for transfers between devices: 332 us -> 60.2 us
  blocking collectives: 34.4 us -> 137 us
  local copies, waits for them, and re-layouts: 45.1 us -> 15.1 us
  starting transfers between devices: 58.8 us -> 31.1 us
  other arithmetic: 23.8 us -> 5.58 us
  between operations: 13.5 us -> 2.61 us
    psum x1 -> x0, waiting for transfers between devices: 212 us -> none  [per_device(): lax.psum((jnp.sum(state_wide, axis=0), jnp.sum(ens_obs.astype(jnp.float32...]
    all_to_all x0 -> x1, blocking collectives: none -> 102 us  [per_device(): recv = lax.all_to_all(pick, 'reg', split_axis=0, concat_axis=0, tiled=True)]
    all_to_all x5 -> x2, waiting for transfers between devices: 120 us -> 60.2 us  [the longest x1 42.4 us: per_device(): rows = lax.all_to_all(recv, 'mem', split_axis=0, concat_axis=0, tiled=True)]
    all_to_all x5 -> x2, starting transfers between devices: 58.8 us -> 31.1 us  [the longest x1 18.4 us: per_device(): lax.all_to_all(ens_state, 'mem', split_axis=1, concat_axis=0, tiled=True)]
    all_to_all x11 -> x1, local copies, waits for them, and re-layouts: 27.4 us -> 2.41 us  [per_device(): lax.all_to_all(ens_state, 'mem', split_axis=1, concat_axis=0, tiled=True)]
    reduce_sum x3 -> x5, other arithmetic: 12.9 us -> 0.95 us  [the longest x2 0.43 us: anomaly(): return (wide - jnp.mean(wide, axis=0, keepdims=True)).astype(jnp.bfloat16)]
    gather x4 -> x0, local copies, waits for them, and re-layouts: 6.8 us -> none  [the longest x1 2.81 us: per_device(): jnp.take(innov.reshape(mem_dev, per_region, BLK), send_ids, axis=1)]
  transfers between devices with their start and end apart: 6 -> 2, of which waited for: 5 -> 2; matrix products, arithmetic and copies ran while one was open for 10% -> 6% of each run, Pallas kernels for 0% -> 0%
where the time goes in v1:
time: 258 us
  blocking collectives  137 us (53%)
  waiting for transfers between devices  60.2 us (23%)
  starting transfers between devices  31.1 us (12%)
  local copies, waits for them, and re-layouts  15.1 us (6%)
  matrix products  6.25 us (2%)
  other arithmetic  5.58 us (2%)
  between operations  2.61 us (1%)
    all_to_all x1, blocking collectives, per_device(): recv = lax.all_to_all(pick, 'reg', split_axis=0, concat_axis=0, tiled=True)  102 us
    all_to_all x1, waiting for transfers between devices, per_device(): rows = lax.all_to_all(recv, 'mem', split_axis=0, concat_axis=0, tiled=True)  42.4 us
    all_to_all x1, blocking collectives, per_device(): lax.all_to_all(increments, 'mem', split_axis=0, concat_axis=1, tiled=True)  34.8 us
    all_to_all x1, starting transfers between devices, per_device(): lax.all_to_all(ens_state, 'mem', split_axis=1, concat_axis=0, tiled=True)  18.4 us
    all_to_all x1, waiting for transfers between devices, per_device(): lax.all_to_all(ens_state, 'mem', split_axis=1, concat_axis=0, tiled=True)  17.8 us
    all_to_all x1, starting transfers between devices, per_device(): rows = lax.all_to_all(recv, 'mem', split_axis=0, concat_axis=0, tiled=True)  12.8 us
  transfers between devices with their start and end apart: 2, of which 2 were waited for; matrix products, arithmetic and copies ran while one was open for 6% of the time, Pallas kernels for 0%

profile of v1, /device:TPU:1, one launch (start us, length us, event | category | flops | bytes accessed | tf_op | source)
XLA Modules:
  0.0 257.7 jit_solution(4132295878379387537)
XLA Ops:
  0.0 2.4 copy.26
  2.4 18.4 %all-to-all-start.2 = ((bf16[16,64,512]{2,0,1:T(8,128)(2,1)}), bf16[16,64,512]{2,0,1:T(8,128)(2,1)S(1)}, u32[]{:S(2)}, u32[]{:S(2)}) async-start(bf16[16,64,512]{2,0,1:T(8,128)(2,1)} %bitcast.51), calls=%async_computation.2 | async-start | bytes 2097152 | tf_op jit(solution)/shard_map/all_to_all | solution.py:45
  20.8 0.9 copy.23
  21.7 0.9 copy.24
  22.6 0.7 fusion.74
  23.3 0.2 convert_reduce_fusion.3
  23.4 2.0 convert_bitcast_fusion.1
  25.4 3.0 %copy.16 = bf16[64,2,16,4,128]{4,3,2,1,0:T(4,128)(2,1)} copy(bf16[64,2,16,4,128]{4,0,3,2,1:T(8,128)(2,1)S(1)} %convert_bitcast_fusion.1) | data formatting | bytes 4194304 | tf_op jit(solution)/shard_map/convert_element_type | solution.py:56
  28.4 2.7 %reshape.129 = bf16[16,128,512]{2,1,0:T(8,128)(2,1)S(1)} reshape(bf16[64,2,16,4,128]{4,3,2,1,0:T(4,128)(2,1)} %copy.16) | data formatting | bytes 4194304 | tf_op jit(solution)/shard_map/reshape | solution.py:57
  31.1 17.8 %all-to-all-done.2 = bf16[16,64,512]{2,0,1:T(8,128)(2,1)S(1)} async-done(((bf16[16,64,512]{2,0,1:T(8,128)(2,1)}), bf16[16,64,512]{2,0,1:T(8,128)(2,1)S(1)}, u32[]{:S(2)}, u32[]{:S(2)}) %all-to-all-start.2) | async-done | bytes 1048608 | tf_op jit(solution)/shard_map/all_to_all | solution.py:45
  48.9 102.0 %all_to_all.36 = bf16[16,128,512]{2,1,0:T(8,128)(2,1)} all-to-all(bf16[16,128,512]{2,1,0:T(8,128)(2,1)S(1)} %reshape.129), channel_id=1, replica_groups=mesh['mem'=64,'reg'=16] {'reg'}, dimensions={0} | all-to-all | bytes 4194304 | tf_op jit(solution)/shard_map/all_to_all | solution.py:58
  151.0 12.8 %all-to-all-start.1 = ((bf16[64,32,512]{2,1,0:T(8,128)(2,1)}), bf16[64,32,512]{2,1,0:T(8,128)(2,1)S(1)}, u32[]{:S(2)}, u32[]{:S(2)}) async-start(bf16[64,32,512]{2,1,0:T(8,128)(2,1)} %bitcast.55), calls=%async_computation.1 | async-start | bytes 4194304 | tf_op jit(solution)/shard_map/all_to_all | solution.py:60
  163.8 0.7 broadcast_compare_fusion
  164.4 0.2 convert_reduce_fusion.2
  164.6 0.2 select_reduce_fusion
  164.8 0.6 fusion.95
  167.9 0.8 constant_dynamic-slice_fusion
  168.7 0.7 constant_dynamic-slice_fusion.4
  169.5 0.1 broadcast_bitcast_fusion
  169.5 0.2 convert_reduce_fusion.1
  169.8 1.2 fusion
  171.0 42.4 %all-to-all-done.1 = bf16[64,32,512]{2,1,0:T(8,128)(2,1)S(1)} async-done(((bf16[64,32,512]{2,1,0:T(8,128)(2,1)}), bf16[64,32,512]{2,1,0:T(8,128)(2,1)S(1)}, u32[]{:S(2)}, u32[]{:S(2)}) %all-to-all-start.1) | async-done | bytes 2097184 | tf_op jit(solution)/shard_map/all_to_all | solution.py:60
  213.4 0.2 convert_reduce_fusion
  213.6 1.1 slice.40
  214.7 1.3 fusion.1
  215.9 4.3 %convolution_convert_fusion = bf16[1024,512]{1,0:T(8,128)(2,1)S(1)} fusion(bf16[1024,512]{1,0:T(8,128)(2,1)} %bitcast.62, bf16[1024,512]{1,0:T(8,128)(2,1)S(1)} %bitcast.60, bf16[1024,512]{1,0:T(8,128)(2,1)} %bitcast.61, f32[512]{0:T(512)S(1)} %broadcast_bitcast_fusion, s32[512]{0:T(512)S(1)} %bitcast.69, s32[512]{0:T(512)S(1)} %bitcast.67, ...), kind=kOutput, calls=%fused_computation.10 | convolution fusion | flops 1084227584 | bytes 4204544 | tf_op jit(solution)/shard_map/dot_general | solution.py:83
  220.2 34.8 %all_to_all.37 = bf16[64,16,512]{2,1,0:T(8,128)(2,1)S(1)} all-to-all(bf16[64,16,512]{2,1,0:T(8,128)(2,1)S(1)} %bitcast.63), channel_id=1, replica_groups=mesh['mem'=64,'reg'=16] {'mem'}, dimensions={0} | all-to-all | bytes 2097152 | tf_op jit(solution)/shard_map/all_to_all | solution.py:86
  255.0 0.3 convert_bitcast_fusion
  255.3 0.0 copy-start
  255.3 0.2 copy.22
  255.5 1.0 copy-done
  256.5 1.1 add_convert_fusion
  (14 shorter events, 0.1 us)
Async XLA Ops:
  0.0 20.8 %copy-start.2 = (bf16[16,16384]{1,0:T(8,128)(2,1)S(1)}, bf16[16,16384]{1,0:T(8,128)(2,1)}, u32[]{:S(2)}) copy-start(bf16[16,16384]{1,0:T(8,128)(2,1)} %param.7) | copy-start | bytes 1572868
  2.4 19.3 %copy-start.3 = (bf16[16,16384]{1,0:T(8,128)(2,1)S(1)}, bf16[16,16384]{1,0:T(8,128)(2,1)}, u32[]{:S(2)}) copy-start(bf16[16,16384]{1,0:T(8,128)(2,1)} %param.8) | copy-start | bytes 1572868
  2.4 46.5 %all-to-all-start.2 = ((bf16[16,64,512]{2,0,1:T(8,128)(2,1)}), bf16[16,64,512]{2,0,1:T(8,128)(2,1)S(1)}, u32[]{:S(2)}, u32[]{:S(2)}) async-start(bf16[16,64,512]{2,0,1:T(8,128)(2,1)} %bitcast.51), calls=%async_computation.2 | async-start | bytes 2097152 | tf_op jit(solution)/shard_map/all_to_all | solution.py:45
  151.0 62.4 %all-to-all-start.1 = ((bf16[64,32,512]{2,1,0:T(8,128)(2,1)}), bf16[64,32,512]{2,1,0:T(8,128)(2,1)S(1)}, u32[]{:S(2)}, u32[]{:S(2)}) async-start(bf16[64,32,512]{2,1,0:T(8,128)(2,1)} %bitcast.55), calls=%async_computation.1 | async-start | bytes 4194304 | tf_op jit(solution)/shard_map/all_to_all | solution.py:60
  213.6 2.3 copy-start.1
  255.3 1.2 copy-start

commit v2 on v1

v2 whole, which is shorter than its diff:
```python
import functools

import jax
import jax.numpy as jnp
from jax import lax
from jax.experimental import pallas as pl
from jax.experimental.pallas import tpu as pltpu
from jax.sharding import PartitionSpec as P

BLK = 128
LOC = 32
SLOTS = 4
WINDOW = 5
LAG = 4
PREP = 9
MESH = pl.DeviceIdType.MESH


def slots_of(target, region, rank):
    k = jnp.arange(target.shape[0], dtype=jnp.int32)
    earlier = (target[None, :] == target[:, None]) & (k[None, :] < k[:, None])
    order = jnp.sum(earlier.astype(jnp.int32), axis=1)
    return ((target[None, :] == region[:, None]) & (order[None, :] == rank[:, None])).astype(jnp.int32)


def taper_weight(dist_sq):
    ratio = jnp.sqrt(dist_sq) / LOC
    clipped = jnp.maximum(ratio, 1.0)
    inner = (((-0.25 * ratio + 0.5) * ratio + 0.625) * ratio - 5.0 / 3.0) * ratio * ratio + 1.0
    outer = (
        ((((ratio / 12.0 - 0.5) * ratio + 0.625) * ratio + 5.0 / 3.0) * ratio - 5.0) * ratio
        + 4.0
        - 2.0 / (3.0 * clipped)
    )
    return jnp.where(ratio <= 1.0, inner, jnp.where(ratio < 2.0, outer, 0.0))


def anomaly(rows):
    wide = rows.astype(jnp.float32)
    return (wide - jnp.mean(wide, axis=0, keepdims=True)).astype(jnp.bfloat16)


def place_of(source, group, groups):
    return lax.div(source, 2) * (2 * groups) + 2 * group + lax.rem(source, 2)


def band_of(place, groups):
    source = 2 * lax.div(place, 2 * groups) + lax.rem(place, 2)
    return source, lax.div(lax.rem(place, 2 * groups), 2)


def loop(start, stop, body):
    def step(i, carry):
        body(i)
        return carry

    lax.fori_loop(start, stop, step, 0)


def gather(n_reg, ids, obs, innov, pack):
    region = lax.axis_index("reg")
    groups = pack.shape[1]

    @functools.partial(loop, 0, n_reg)
    def _(shift):
        to = lax.rem(region + shift, n_reg)
        for c in range(groups * SLOTS):
            lanes = pl.ds(pl.multiple_of(ids[to * (groups * SLOTS) + c] * BLK, BLK), BLK)
            at = pl.ds(c % SLOTS * BLK, BLK)
            pack[shift, c // SLOTS, 0, :, at] = obs[:, lanes]
            pack[shift, c // SLOTS, 1, :, at] = innov[:, lanes]


def kernel(
    n_mem, n_reg, state, pack, rows_xy, obs_xy, present, returned, land,
    rows, rows_t, pair, taper, tiles, incr,
    z_send, z_recv, s_send, s_recv, f_send, f_recv, r_send, r_recv,
):
    mine, region = lax.axis_index("mem"), lax.axis_index("reg")
    groups = n_mem // n_reg
    my_source, my_group = band_of(mine, groups)
    per = state.shape[0]
    members, wide = rows.shape
    my_rows = pl.ds(pl.multiple_of(mine * per, per), per)

    def columns(band):
        return pl.ds(pl.multiple_of(band * wide, wide), wide)

    def remote(src, dst, send, recv, mem, reg):
        return pltpu.make_async_remote_copy(
            src_ref=src, dst_ref=dst, send_sem=send, recv_sem=recv, device_id=(mem, reg), device_id_type=MESH
        )

    barrier = pltpu.get_barrier_semaphore()

    @functools.partial(loop, 1, n_mem)
    def _(s):
        pl.semaphore_signal(barrier, inc=1, device_id=(lax.rem(mine + s, n_mem), region), device_id_type=MESH)

    @functools.partial(loop, 1, n_reg)
    def _(s):
        pl.semaphore_signal(barrier, inc=1, device_id=(mine, lax.rem(region + s, n_reg)), device_id_type=MESH)

    def shift_of(k):
        half = lax.div(k + 1, 2)
        return half + (1 - lax.rem(k, 2)) * (n_reg - 2 * half) * jnp.minimum(k, 1)

    def along_z(shift, group):
        return remote(
            pack.at[shift, group], land.at[shift, group], z_send.at[shift, group], z_recv.at[shift, group],
            mine, lax.rem(region + shift, n_reg),
        )

    def send_z(k):
        shift = shift_of(k)
        for group in range(groups):
            along_z(shift, group).start()

    pl.semaphore_wait(barrier, n_mem + n_reg - 2)
    loop(1, min(WINDOW, n_reg - 1) + 1, send_z)

    @functools.partial(loop, 1, n_mem)
    def _(s):
        to = lax.rem(mine + s, n_mem)
        source, group = band_of(to, groups)
        remote(state.at[:, columns(source * groups + group)], rows.at[my_rows], s_send, s_recv, to, region).start()

    pltpu.make_async_copy(state.at[:, columns(my_source * groups + my_group)], rows.at[my_rows], s_recv).start()

    def make_taper(i):
        at = pl.ds(pl.multiple_of(i * BLK, BLK), BLK)
        dx = rows_xy[at, 0:1] - obs_xy[0:1, :]
        dy = rows_xy[at, 1:2] - obs_xy[1:2, :]
        near = taper_weight((dx * dx + dy * dy).astype(jnp.float32))
        taper[at, :] = near * (present[0:1, :] / (members - 1))

    loop(0, wide // BLK, make_taper)

    def forward(shift, held):
        source = lax.rem(region + n_reg - shift, n_reg)
        for group in range(groups):
            to = place_of(source, group, groups)

            if held is land:
                along_z(shift, group).wait_recv()

            @pl.when(to != mine)
            def _():
                remote(held.at[shift, group], pair.at[:, my_rows], f_send, f_recv, to, region).start()

            @pl.when(to == mine)
            def _():
                pltpu.make_async_copy(held.at[shift, group], pair.at[:, my_rows], f_recv).start()

    def prepare():
        pltpu.make_async_copy(rows, rows, s_recv).wait()

        @functools.partial(loop, 0, wide // BLK)
        def _(i):
            at = pl.ds(pl.multiple_of(i * BLK, BLK), BLK)
            rows_t[at, :] = anomaly(rows[:, at]).astype(jnp.float32).T.astype(jnp.bfloat16)

    def update():
        pltpu.make_async_copy(pair, pair, f_recv).wait()
        half = wide // 2

        @functools.partial(loop, 0, 2)
        def _(i):
            at = pl.ds(pl.multiple_of(i * half, half), half)
            cov = jnp.dot(rows_t[...], anomaly(pair[0, :, at]), preferred_element_type=jnp.float32)
            tiles[:, at] = (cov * taper[:, at]).astype(jnp.bfloat16)

        share = n_mem // 4

        @functools.partial(loop, 0, 4)
        def _(i):
            part = lax.rem(lax.div(mine, share) + i, 4)
            at = pl.ds(pl.multiple_of(part * (share * per), share * per), share * per)
            incr[at, :] = lax.dot_general(
                pair[1, at, :], tiles[...], (((1,), (1,)), ((), ())), preferred_element_type=jnp.float32
            ).astype(jnp.bfloat16)

            @functools.partial(loop, 0, share)
            def _(s):
                to = part * share + lax.rem(mine + s, share)
                src = incr.at[pl.ds(pl.multiple_of(to * per, per), per)]
                dst = returned.at[:, columns(my_source * groups + my_group)]

                @pl.when(to != mine)
                def _():
                    remote(src, dst, r_send, r_recv, to, region).start()

                @pl.when(to == mine)
                def _():
                    pltpu.make_async_copy(src, dst, r_recv).start()

    my_shift = lax.rem(region + n_reg - my_source, n_reg)
    ahead = jnp.minimum(my_shift, n_reg - my_shift)
    my_step = 2 * ahead - jnp.where(my_shift == ahead, 1, 0) * jnp.minimum(ahead, 1) + LAG
    prep_step = jnp.minimum(my_step, PREP)

    forward(0, pack)

    @functools.partial(loop, 1, n_reg + LAG)
    def _(k):
        @pl.when(k + WINDOW < n_reg)
        def _():
            send_z(k + WINDOW)

        @pl.when(k < n_reg)
        def _():
            forward(shift_of(k), land)

        pl.when(k == prep_step)(prepare)
        pl.when(k == my_step)(update)

    def drain(k):
        for group in range(groups):
            along_z(shift_of(k), group).wait_send()

    loop(1, n_reg, drain)
    sent = rows.at[pl.ds(0, (n_mem - 1) * per)]
    pltpu.make_async_copy(sent, sent, s_send).wait()
    pltpu.make_async_copy(sent, sent, r_send).wait()
    both = pair.at[:, pl.ds(0, (n_mem - 1) * per)]
    pltpu.make_async_copy(both, both, f_send).wait()
    pltpu.make_async_copy(returned, returned, r_recv).wait()


def per_device(ens_state, ens_obs, innov, state_coord, obs_coord, obs_routes):
    n_reg, n_mem = lax.axis_size("reg"), lax.axis_size("mem")
    region, mine = lax.axis_index("reg"), lax.axis_index("mem")
    per = ens_state.shape[0]
    per_region = ens_obs.shape[1] // BLK
    groups = n_mem // n_reg
    capacity = SLOTS * groups
    wide = ens_state.shape[1] // n_mem
    paired = SLOTS * BLK
    routes = obs_routes[:, 0]
    k = jnp.arange(per_region, dtype=jnp.int32)
    q = jnp.arange(n_reg * capacity, dtype=jnp.int32)
    target = lax.dynamic_slice_in_dim(routes, region * per_region, per_region)
    ids = jnp.sum(slots_of(target, q // capacity, q % capacity) * k, axis=1)
    source, group = band_of(mine, groups)
    theirs = lax.dynamic_slice_in_dim(routes, source * per_region, per_region)
    here = slots_of(
        theirs, jnp.full((SLOTS,), region), group * SLOTS + jnp.arange(SLOTS, dtype=jnp.int32)
    )
    blocks = source * per_region + jnp.sum(here * k, axis=1)
    present = jnp.repeat(jnp.sum(here, axis=1), BLK).astype(jnp.float32)[None, :]
    obs_xy = jnp.concatenate(
        [lax.dynamic_slice_in_dim(obs_coord, blocks[s] * BLK, BLK, 1) for s in range(SLOTS)], axis=1
    )
    rows_xy = lax.dynamic_slice_in_dim(state_coord, (source * groups + group) * wide, wide, 1).T
    members = per * n_mem
    vmem = pl.BlockSpec(memory_space=pltpu.VMEM)
    half = jnp.bfloat16
    smem = pl.BlockSpec(memory_space=pltpu.SMEM)
    anywhere = pl.BlockSpec(memory_space=pl.ANY)
    pack = pl.pallas_call(
        functools.partial(gather, n_reg),
        out_shape=jax.ShapeDtypeStruct((n_reg, groups, 2, per, paired), half),
        in_specs=[smem, vmem, vmem],
        out_specs=vmem,
        compiler_params=pltpu.CompilerParams(vmem_limit_bytes=16 * 2**20),
    )(ids, ens_obs, innov)
    returned = pl.pallas_call(
        functools.partial(kernel, n_mem, n_reg),
        out_shape=jax.ShapeDtypeStruct(ens_state.shape, half),
        in_specs=[anywhere, anywhere, vmem, vmem, vmem],
        out_specs=anywhere,
        scratch_shapes=[
            pltpu.VMEM((n_reg, groups, 2, per, paired), half),
            pltpu.VMEM((members, wide), half),
            pltpu.VMEM((wide, members), half),
            pltpu.VMEM((2, members, paired), half),
            pltpu.VMEM((wide, paired), jnp.float32),
            pltpu.VMEM((wide, paired), half),
            pltpu.VMEM((members, wide), half),
            pltpu.SemaphoreType.DMA((n_reg, groups)),
            pltpu.SemaphoreType.DMA((n_reg, groups)),
        ]
        + [pltpu.SemaphoreType.DMA] * 6,
        compiler_params=pltpu.CompilerParams(
            collective_id=0, has_side_effects=True, vmem_limit_bytes=48 * 2**20
        ),
    )(ens_state, pack, rows_xy, obs_xy, present)
    return (ens_state.astype(jnp.float32) + returned.astype(jnp.float32)).astype(jnp.bfloat16)


def solution(mesh):
    return jax.shard_map(
        per_device,
        mesh=mesh,
        in_specs=(P("mem", "reg"), P("mem", "reg"), P("mem", "reg"), P(None, "reg"), P(), P()),
        out_specs=P("mem", "reg"),
        check_vma=False,
    )
```

time: 258 us -> 199 us (0.77)
  Pallas kernels: 0 us -> 189 us
  blocking collectives: 137 us -> 0 us
  waiting for transfers between devices: 60.2 us -> 0 us
  starting transfers between devices: 31.1 us -> 0 us
  local copies, waits for them, and re-layouts: 15.1 us -> 4.49 us
  matrix products: 6.25 us -> 0 us
  other arithmetic: 5.58 us -> 2.63 us
    pallas_call x0 -> x2, Pallas kernels: none -> 189 us  [the longest x1 188 us: per_device(): pl.pallas_call(functools.partial(kernel, n_mem, n_reg), out_shape=jax.Sha...]
    all_to_all x2 -> x0, blocking collectives: 137 us -> none  [the longest x1 102 us: per_device(): recv = lax.all_to_all(pick, 'reg', split_axis=0, concat_axis=0, tiled=True)]
    all_to_all x2 -> x0, waiting for transfers between devices: 60.2 us -> none  [the longest x1 42.4 us: per_device(): rows = lax.all_to_all(recv, 'mem', split_axis=0, concat_axis=0, tiled=True)]
    all_to_all x2 -> x0, starting transfers between devices: 31.1 us -> none  [the longest x1 18.4 us: per_device(): lax.all_to_all(ens_state, 'mem', split_axis=1, concat_axis=0, tiled=True)]
    dot_general x2 -> x0, matrix products: 6.25 us -> none  [the longest x1 4.28 us: per_device(): lax.dot_general(innov_rows, tiles, (((1,), (1,)), ((), ())), preferred_el...]
    convert_element_type x3 -> x0, local copies, waits for them, and re-layouts: 3.23 us -> none  [the longest x1 2.97 us: per_device(): pick = jnp.einsum('gsk,amkx->gamsx', hot.reshape(bands, SLOTS, per_region...]
    reshape x1 -> x0, local copies, waits for them, and re-layouts: 2.75 us -> none  [per_device(): pick = pick.reshape(regions, bands // regions * 2 * mem_dev, wide)]
  transfers between devices with their start and end apart: 2 -> 0, of which waited for: 2 -> 0; matrix products, arithmetic and copies ran while one was open for 6% -> 0% of each run, Pallas kernels for 0% -> 0%
where the time goes in v2:
time: 199 us
  Pallas kernels  189 us (95%)
  local copies, waits for them, and re-layouts  4.49 us (2%)
  between operations  2.64 us (1%)
  other arithmetic  2.63 us (1%)
    pallas_call x1, Pallas kernels, per_device(): pl.pallas_call(functools.partial(kernel, n_mem, n_reg), out_shape=jax.Sha...  188 us

profile of v2, /device:TPU:1, one launch (start us, length us, event | category | flops | bytes accessed | tf_op | source)
XLA Modules:
  0.0 198.7 jit_solution(2306187700400312146)
XLA Ops:
  0.0 0.0 copy-start
  0.0 0.0 copy-start.1
  0.0 0.8 fusion.4
  0.8 0.7 broadcast_compare_fusion
  1.4 0.2 convert_reduce_fusion
  1.6 0.2 convert_reduce_fusion.2
  1.8 0.2 convert_reduce_fusion.1
  2.0 0.1 broadcast_in_dim.2
  2.1 0.7 fusion.7
  5.3 0.7 constant_dynamic-slice_fusion.3
  6.0 0.2 select_reduce_fusion.ids
  6.2 0.0 copy-done
  6.3 0.1 copy.9
  6.4 0.0 copy-start.2
  6.4 1.0 copy-done.2
  7.5 0.0 copy-start.3
  7.5 1.0 copy-done.3
  8.5 1.2 shard_map.64.pack
  9.8 0.0 copy-done.1
  9.8 187.7 %shard_map.65 = bf16[16,32768]{1,0:T(8,128)(2,1)S(1)} custom-call(bf16[16,32768]{1,0:T(8,128)(2,1)S(1)} %copy-done.1, bf16[16,4,2,16,512]{4,3,2,1,0:T(8,128)(2,1)S(1)} %shard_map.64.pack, s32[512,2]{1,0:T(8,128)S(1)} %bitcast.11, s32[2,512]{1,0:T(2,128)S(1)} %pad_add_fusion.obs_xy, f32[1,512]{1,0:T(1,128)S(1)} %bitcast.12), custom_call_target="tpu_custom_call" | custom-call | tf_op jit(solution)/shard_map/pallas_call | solution.py:267
  197.4 1.2 add_convert_fusion
  (6 shorter events, 0.0 us)
Async XLA Ops:
  0.0 6.2 %copy-start = (s32[2,32768]{1,0:T(2,128)S(1)}, s32[2,32768]{1,0:T(2,128)}, u32[]{:S(2)}) copy-start(s32[2,32768]{1,0:T(2,128)} %param.9) | copy-start | bytes 786436
  0.0 9.8 %copy-start.1 = (bf16[16,32768]{1,0:T(8,128)(2,1)S(1)}, bf16[16,32768]{1,0:T(8,128)(2,1)}, u32[]{:S(2)}) copy-start(bf16[16,32768]{1,0:T(8,128)(2,1)} %state.1) | copy-start | bytes 3145732
  6.4 1.0 copy-start.2
  7.5 1.0 copy-start.3

commit v3 on v2

v3 whole, which is shorter than its diff:
```python
import functools

import jax
import jax.numpy as jnp
from jax import lax
from jax.experimental import pallas as pl
from jax.experimental.pallas import tpu as pltpu
from jax.sharding import PartitionSpec as P

BLK = 128
LOC = 32
SLOTS = 4
WINDOW = 20
LAG = 12
PREP = 26
STATES = 3
MESH = pl.DeviceIdType.MESH


def taper_weight(dist_sq):
    ratio = jnp.sqrt(dist_sq) / LOC
    clipped = jnp.maximum(ratio, 1.0)
    inner = (((-0.25 * ratio + 0.5) * ratio + 0.625) * ratio - 5.0 / 3.0) * ratio * ratio + 1.0
    outer = (
        ((((ratio / 12.0 - 0.5) * ratio + 0.625) * ratio + 5.0 / 3.0) * ratio - 5.0) * ratio
        + 4.0
        - 2.0 / (3.0 * clipped)
    )
    return jnp.where(ratio <= 1.0, inner, jnp.where(ratio < 2.0, outer, 0.0))


def anomaly(rows):
    wide = rows.astype(jnp.float32)
    return (wide - jnp.mean(wide, axis=0, keepdims=True)).astype(jnp.bfloat16)


def place_of(source, group, groups):
    y = lax.div(source, 2)
    x = 2 * lax.rem(source, 2) + lax.rem(lax.div(group, 2) + y, 2)
    return y * (2 * groups) + 2 * x + lax.rem(group, 2)


def band_of(place, groups):
    y = lax.div(place, 2 * groups)
    x = lax.div(lax.rem(place, 2 * groups), 2)
    return 2 * y + lax.div(x, 2), 2 * lax.rem(x + y, 2) + lax.rem(place, 2)


def loop(start, stop, body):
    def step(i, carry):
        body(i)
        return carry

    lax.fori_loop(start, stop, step, 0)


def stage(
    n_mem, n_reg, routes, obs, innov, state_xy, obs_xy, pack, rows_at, obs_at, present,
    obs_in, innov_in, ids, counts, mine_ids, sems,
):
    mine, region = lax.axis_index("mem"), lax.axis_index("reg")
    groups, per_region, wide = n_mem // n_reg, routes.shape[1], rows_at.shape[1]
    capacity = groups * SLOTS
    source, group = band_of(mine, groups)
    band = source * groups + group
    copies = [
        pltpu.make_async_copy(obs, obs_in, sems.at[0]),
        pltpu.make_async_copy(innov, innov_in, sems.at[1]),
        pltpu.make_async_copy(
            state_xy.at[:, pl.ds(pl.multiple_of(band * wide, wide), wide)], rows_at, sems.at[2]
        ),
    ]
    for copy in copies:
        copy.start()

    @functools.partial(loop, 0, n_reg)
    def _(r):
        counts[r] = 0
        for c in range(capacity):
            ids[r * capacity + c] = 0

    for s in range(SLOTS):
        mine_ids[s] = 0

    def tally(k, seen):
        to = routes[region, k]
        at = counts[to]
        ids[to * capacity + at] = k
        counts[to] = at + 1
        hit = routes[source, k] == region
        slot = seen - group * SLOTS

        @pl.when(hit & (slot >= 0) & (slot < SLOTS))
        def _():
            mine_ids[slot] = k

        return seen + hit.astype(jnp.int32)

    total = lax.fori_loop(0, per_region, tally, 0)
    for s in range(SLOTS):
        block = source * per_region + mine_ids[s]
        at = pl.ds(s * BLK, BLK)
        copy = pltpu.make_async_copy(
            obs_xy.at[:, pl.ds(pl.multiple_of(block * BLK, BLK), BLK)], obs_at.at[:, at], sems.at[3 + s]
        )
        copy.start()
        copies.append(copy)
        filled = (group * SLOTS + s < total).astype(jnp.int32)
        present[:, at] = jnp.full((1, BLK), filled, jnp.int32).astype(jnp.float32)
    copies[0].wait()
    copies[1].wait()

    @functools.partial(loop, 0, n_reg)
    def _(shift):
        to = lax.rem(region + shift, n_reg)
        for c in range(capacity):
            lanes = pl.ds(pl.multiple_of(ids[to * capacity + c] * BLK, BLK), BLK)
            at = pl.ds(c % SLOTS * BLK, BLK)
            pack[shift, c // SLOTS, 0, :, at] = obs_in[:, lanes]
            pack[shift, c // SLOTS, 1, :, at] = innov_in[:, lanes]

    for copy in copies[2:]:
        copy.wait()


def batched(start, stop, body, most=8):
    size = max(n for n in range(1, most + 1) if (stop - start) % n == 0)

    @functools.partial(loop, 0, (stop - start) // size)
    def _(i):
        for j in range(size):
            body(start + i * size + j)


def kernel(
    n_mem, n_reg, state, pack, rows_xy, obs_xy, present, returned, land,
    rows, rows_t, pair, taper, tiles, incr,
    z_send, z_recv, s_send, s_recv, f_send, f_recv, r_send, r_recv,
):
    mine, region = lax.axis_index("mem"), lax.axis_index("reg")
    groups = n_mem // n_reg
    my_source, my_group = band_of(mine, groups)
    per = state.shape[0]
    members, wide = rows.shape
    my_rows = pl.ds(pl.multiple_of(mine * per, per), per)

    def columns(band):
        return pl.ds(pl.multiple_of(band * wide, wide), wide)

    def remote(src, dst, send, recv, mem, reg):
        return pltpu.make_async_remote_copy(
            src_ref=src, dst_ref=dst, send_sem=send, recv_sem=recv, device_id=(mem, reg), device_id_type=MESH
        )

    barrier = pltpu.get_barrier_semaphore()

    @functools.partial(loop, 1, n_mem)
    def _(s):
        pl.semaphore_signal(barrier, inc=1, device_id=(lax.rem(mine + s, n_mem), region), device_id_type=MESH)

    @functools.partial(loop, 1, n_reg)
    def _(s):
        pl.semaphore_signal(barrier, inc=1, device_id=(mine, lax.rem(region + s, n_reg)), device_id_type=MESH)

    turn = 2 * lax.rem(lax.div(mine, 2), groups) + lax.div(mine, 2 * groups)

    def piece_of(k):
        at = lax.rem(k, n_reg)
        near = lax.rem(lax.div(at, 2) + turn, n_reg // 2)
        other = jnp.where(near == 0, n_reg // 2, n_reg - near)
        return lax.div(k, n_reg), jnp.where(lax.rem(at, 2) == 0, near, other)

    def along_z(group, shift):
        return remote(
            pack.at[shift, group], land.at[shift, group], z_send.at[shift, group], z_recv.at[shift, group],
            mine, lax.rem(region + shift, n_reg),
        )

    def stays(group, shift):
        return pltpu.make_async_copy(pack.at[shift, group], land.at[shift, group], z_recv.at[shift, group])

    def send_z(k):
        group, shift = piece_of(k)

        @pl.when(shift > 0)
        def _():
            along_z(group, shift).start()

        @pl.when(shift == 0)
        def _():
            stays(group, shift).start()

    pl.semaphore_wait(barrier, n_mem + n_reg - 2)
    steps = n_reg * groups
    loop(0, min(WINDOW, steps), send_z)
    pltpu.make_async_copy(state.at[:, columns(my_source * groups + my_group)], rows.at[my_rows], s_recv).start()

    def nth(s):
        half = lax.div(s + 1, 2)
        return lax.rem(mine + jnp.where(lax.rem(s, 2) == 1, half, n_mem - half), n_mem)

    def send_state(s):
        to = nth(s)
        source, group = band_of(to, groups)
        remote(state.at[:, columns(source * groups + group)], rows.at[my_rows], s_send, s_recv, to, region).start()

    def make_taper(i):
        at = pl.ds(pl.multiple_of(i * BLK, BLK), BLK)
        mine_xy = [
            jnp.broadcast_to(rows_xy[a : a + 1, at].astype(jnp.float32), (BLK, BLK)).T[:, 0:1] for a in range(2)
        ]
        dx = mine_xy[0] - obs_xy[0:1, :].astype(jnp.float32)
        dy = mine_xy[1] - obs_xy[1:2, :].astype(jnp.float32)
        taper[at, :] = taper_weight(dx * dx + dy * dy) * (present[0:1, :] / (members - 1))

    loop(0, wide // BLK, make_taper)

    def forward(k):
        group, shift = piece_of(k)
        source = lax.rem(region + n_reg - shift, n_reg)
        to = place_of(source, group, groups)
        stays(group, shift).wait()

        @pl.when(to != mine)
        def _():
            remote(land.at[shift, group], pair.at[:, my_rows], f_send, f_recv, to, region).start()

        @pl.when(to == mine)
        def _():
            pltpu.make_async_copy(land.at[shift, group], pair.at[:, my_rows], f_recv).start()

    def prepare():
        pltpu.make_async_copy(rows, rows, s_recv).wait()

        @functools.partial(loop, 0, wide // BLK)
        def _(i):
            at = pl.ds(pl.multiple_of(i * BLK, BLK), BLK)
            rows_t[at, :] = anomaly(rows[:, at]).astype(jnp.float32).T.astype(jnp.bfloat16)

    def update():
        pltpu.make_async_copy(pair, pair, f_recv).wait()
        half = wide // 2

        @functools.partial(loop, 0, 2)
        def _(i):
            at = pl.ds(pl.multiple_of(i * half, half), half)
            cov = jnp.dot(rows_t[...], anomaly(pair[0, :, at]), preferred_element_type=jnp.float32)
            tiles[:, at] = (cov * taper[:, at]).astype(jnp.bfloat16)

        part = members // 4

        @functools.partial(loop, 0, 4)
        def _(i):
            at = pl.ds(pl.multiple_of(i * part, part), part)
            incr[at, :] = lax.dot_general(
                pair[1, at, :], tiles[...], (((1,), (1,)), ((), ())), preferred_element_type=jnp.float32
            ).astype(jnp.bfloat16)

        dst = returned.at[:, columns(my_source * groups + my_group)]
        pltpu.make_async_copy(incr.at[my_rows], dst, r_recv).start()

        def give(s):
            to = nth(s)
            remote(incr.at[pl.ds(pl.multiple_of(to * per, per), per)], dst, r_send, r_recv, to, region).start()

        batched(1, n_mem, give)

    my_step = (my_group + 1) * n_reg + LAG

    @functools.partial(loop, 0, steps + LAG + 1)
    def _(k):
        @pl.when(k + WINDOW < steps)
        def _():
            send_z(k + WINDOW)

        for i in range(STATES):
            s = STATES * k + i + 1

            @pl.when(s < n_mem)
            def _():
                send_state(s)

        pl.when(k < steps)(lambda: forward(k))
        pl.when(k == jnp.minimum(PREP, my_step))(prepare)
        pl.when(k == my_step)(update)

    @functools.partial(loop, 0, groups)
    def _(group):
        loop(1, n_reg, lambda shift: along_z(group, shift).wait_send())

    sent = rows.at[pl.ds(0, (n_mem - 1) * per)]
    pltpu.make_async_copy(sent, sent, s_send).wait()
    pltpu.make_async_copy(sent, sent, r_send).wait()
    both = pair.at[:, pl.ds(0, (n_mem - 1) * per)]
    pltpu.make_async_copy(both, both, f_send).wait()
    pltpu.make_async_copy(returned, returned, r_recv).wait()


def per_device(ens_state, ens_obs, innov, state_coord, obs_coord, obs_routes):
    n_reg, n_mem = lax.axis_size("reg"), lax.axis_size("mem")
    per = ens_state.shape[0]
    per_region = ens_obs.shape[1] // BLK
    groups = n_mem // n_reg
    capacity = SLOTS * groups
    wide = ens_state.shape[1] // n_mem
    paired = SLOTS * BLK
    members = per * n_mem
    vmem = pl.BlockSpec(memory_space=pltpu.VMEM)
    hbm = pl.BlockSpec(memory_space=pltpu.HBM)
    anywhere = pl.BlockSpec(memory_space=pl.ANY)
    half = jnp.bfloat16
    pack, rows_xy, obs_xy, present = pl.pallas_call(
        functools.partial(stage, n_mem, n_reg),
        out_shape=[
            jax.ShapeDtypeStruct((n_reg, groups, 2, per, paired), half),
            jax.ShapeDtypeStruct((2, wide), jnp.int32),
            jax.ShapeDtypeStruct((2, paired), jnp.int32),
            jax.ShapeDtypeStruct((1, paired), jnp.float32),
        ],
        in_specs=[pl.BlockSpec(memory_space=pltpu.SMEM), hbm, hbm, hbm, hbm],
        out_specs=[vmem] * 4,
        scratch_shapes=[
            pltpu.VMEM(ens_obs.shape, half),
            pltpu.VMEM(innov.shape, half),
            pltpu.SMEM((n_reg * capacity,), jnp.int32),
            pltpu.SMEM((n_reg,), jnp.int32),
            pltpu.SMEM((SLOTS,), jnp.int32),
            pltpu.SemaphoreType.DMA((3 + SLOTS,)),
        ],
        compiler_params=pltpu.CompilerParams(vmem_limit_bytes=58 * 2**20),
    )(obs_routes.reshape(n_reg, per_region), ens_obs, innov, state_coord, obs_coord)
    returned = pl.pallas_call(
        functools.partial(kernel, n_mem, n_reg),
        out_shape=jax.ShapeDtypeStruct(ens_state.shape, half),
        in_specs=[anywhere, anywhere, vmem, vmem, vmem],
        out_specs=anywhere,
        scratch_shapes=[
            pltpu.VMEM((n_reg, groups, 2, per, paired), half),
            pltpu.VMEM((members, wide), half),
            pltpu.VMEM((wide, members), half),
            pltpu.VMEM((2, members, paired), half),
            pltpu.VMEM((wide, paired), jnp.float32),
            pltpu.VMEM((wide, paired), half),
            pltpu.VMEM((members, wide), half),
            pltpu.SemaphoreType.DMA((n_reg, groups)),
            pltpu.SemaphoreType.DMA((n_reg, groups)),
        ]
        + [pltpu.SemaphoreType.DMA] * 6,
        compiler_params=pltpu.CompilerParams(
            collective_id=0, has_side_effects=True, vmem_limit_bytes=58 * 2**20
        ),
    )(ens_state, pack, rows_xy, obs_xy, present)
    return (ens_state.astype(jnp.float32) + returned.astype(jnp.float32)).astype(jnp.bfloat16)


def solution(mesh):
    return jax.shard_map(
        per_device,
        mesh=mesh,
        in_specs=(P("mem", "reg"), P("mem", "reg"), P("mem", "reg"), P(None, "reg"), P(), P()),
        out_specs=P("mem", "reg"),
        check_vma=False,
    )
```

time: 199 us -> 169 us (0.85)
  Pallas kernels: 189 us -> 168 us
  local copies, waits for them, and re-layouts: 4.49 us -> 0.01 us
  between operations: 2.64 us -> 0.03 us
    pallas_call x1, Pallas kernels: 188 us -> 163 us  [per_device(): pl.pallas_call(functools.partial(kernel, n_mem, n_reg), out_shape=jax.Sha...]
    pallas_call x1, Pallas kernels: 1.25 us -> 5.34 us  [per_device(): pl.pallas_call(functools.partial(stage, n_mem, n_reg), out_shape=[jax.Sha...]
    unnamed x9 -> x2, local copies, waits for them, and re-layouts: 2.23 us -> 0.01 us
where the time goes in v3:
time: 169 us; the launch traced here: 170 us
  Pallas kernels  168 us (99%)
  other arithmetic  2.43 us (1%)
    pallas_call x1, Pallas kernels, per_device(): pl.pallas_call(functools.partial(kernel, n_mem, n_reg), out_shape=jax.Sha...  163 us
    pallas_call x1, Pallas kernels, per_device(): pl.pallas_call(functools.partial(stage, n_mem, n_reg), out_shape=[jax.Sha...  5.34 us

profile of v3, /device:TPU:1, one launch (start us, length us, event | category | flops | bytes accessed | tf_op | source)
XLA Modules:
  0.0 170.5 jit_solution(4367855174919208188)
XLA Ops:
  0.0 5.3 %shard_map.64 = (bf16[16,4,2,16,512]{4,3,2,1,0:T(8,128)(2,1)}, s32[2,512]{1,0:T(2,128)}, s32[2,512]{1,0:T(2,128)}, f32[1,512]{1,0:T(1,128)}) custom-call(s32[16,128]{1,0:T(8,128)} %bitcast.1, bf16[16,16384]{1,0:T(8,128)(2,1)} %obs.1, bf16[16,16384]{1,0:T(8,128)(2,1)} %innov.1, s32[2,32768]{1,0:T(2,128)} %state_xy.1, s32[2,262144]{1,0:T(2,128)} %obs_xy.1), custom_call_target="tpu_custom_call" | custom-call | tf_op jit(solution)/shard_map/pallas_call | solution.py:312
  5.4 0.0 copy-start
  5.4 162.7 %shard_map.65 = bf16[16,32768]{1,0:T(8,128)(2,1)} custom-call(bf16[16,32768]{1,0:T(8,128)(2,1)} %state.1, bf16[16,4,2,16,512]{4,3,2,1,0:T(8,128)(2,1)} %get-tuple-element.9.pack, s32[2,512]{1,0:T(2,128)} %get-tuple-element.10.rows_xy, s32[2,512]{1,0:T(2,128)} %get-tuple-element.11.obs_xy, f32[1,512]{1,0:T(1,128)} %get-tuple-element.12.present), custom_call_target="tpu_custom_call" | custom-call | tf_op jit(solution)/shard_map/pallas_call | solution.py:332
  168.0 0.0 copy-done
  168.0 2.4 %add_convert_fusion = bf16[16,32768]{1,0:T(8,128)(2,1)} fusion(bf16[16,32768]{1,0:T(8,128)(2,1)} %shard_map.65, bf16[16,32768]{1,0:T(8,128)(2,1)S(1)} %copy-done), kind=kLoop, calls=%fused_computation | loop fusion | flops 2097152 | bytes 3145728 | tf_op jit(solution)/shard_map/convert_element_type | solution.py:353
Async XLA Ops:
  5.4 162.7 %copy-start = (bf16[16,32768]{1,0:T(8,128)(2,1)S(1)}, bf16[16,32768]{1,0:T(8,128)(2,1)}, u32[]{:S(2)}) copy-start(bf16[16,32768]{1,0:T(8,128)(2,1)} %state.1) | copy-start | bytes 3145732
